TPU v7x, 128 devices: a whole 4x4x4 slice. The times are simulated.
128 devices in a mesh: fsdp: 32 (over y, x, z_hi), tp: 4 (over z_lo, core).
Axes of the slice: x: 4, y: 4, z: 4 (z_hi: 2, z_lo: 2; z = z_hi * 2 + z_lo), core: 2. Of those that a mesh axis runs over, the one named last changes fastest.
Arguments:
- activations: bfloat16 [65536, 5120], P(('fsdp', 'tp')), may hold values from -24 to 24
- grad_out: bfloat16 [65536, 1024], P(('fsdp', 'tp')), may hold values from -6 to 6
- master_w: float32 [5120, 1024], P(('fsdp', 'tp')), may hold values from -0.078125 to 0.078125
- embed_table: bfloat16 [151936, 5120], P(('fsdp', 'tp')), may hold values from -6 to 6
- token_ids: int32 [256], replicated, may hold values from 0 to 151935
- queries: bfloat16 [256, 8192], P('fsdp', 'tp'), may hold values from -30 to 30
- cache_keys: bfloat16 [256, 512, 1024], P('fsdp', None, 'tp'), may hold values from -6 to 6
- cache_values: bfloat16 [256, 512, 1024], P('fsdp', None, 'tp'), may hold values from -6 to 6
- new_key: bfloat16 [256, 1024], P('fsdp', 'tp'), may hold values from -6 to 6
- first_value: bfloat16 [256, 1024], P('fsdp', 'tp'), may hold values from -6 to 6
- residual_mix: float32 [8], P('tp'), may hold values from 0.2 to 0.8
- lengths: int32 [256], P('fsdp'), may hold values from 1 to 512, 65536 in all
Outputs:
- w_next: float32 [5120, 1024], P(('fsdp', 'tp'))
- new_value: bfloat16 [256, 1024], P('fsdp', 'tp')
- attended: bfloat16 [256, 8192], P('fsdp', 'tp')
Inputs may be any that keep to these rules, and one draw needn't show every extreme that they name: `lengths`: some row holds exactly 512 positions.
All inputs are finite; a program needn't handle non-finite values. No bound on the sum of `lengths` on one device may be relied on, other than what follows from the above.
Results may differ from a plain program's by a relative error of at most 0.006.
Values may be sent and summed in bfloat16 or wider, within the bound.
A program may use at most 128 MiB of HBM per device.

v0:
```python
import math

import jax
import jax.numpy as jnp
from jax import lax
from jax.sharding import PartitionSpec as P

HEADS = 64
KV = 8
HD = 128


def per_device(
    activations,
    grad_out,
    master_w,
    embed_table,
    token_ids,
    queries,
    cache_keys,
    cache_values,
    new_key,
    first_value,
    residual_mix,
    lengths,
):
    count_fsdp = lax.axis_size("fsdp")
    count_tp = lax.axis_size("tp")
    devices_all = count_fsdp * count_tp
    width = activations.shape[1]
    tokens_total = activations.shape[0] * devices_all
    grad_w = lax.psum_scatter(
        lax.dot_general(
            activations, grad_out, (((0,), (0,)), ((), ())), preferred_element_type=jnp.float32
        ),
        ("fsdp", "tp"),
        scatter_dimension=0,
        tiled=True,
    )
    coef = 1.0 / math.sqrt(tokens_total * width)
    w_next = master_w - coef * grad_w
    w_roll = w_next.astype(jnp.bfloat16)
    vocab_local = embed_table.shape[0]
    vocab_start = (lax.axis_index("fsdp") * count_tp + lax.axis_index("tp")) * vocab_local
    picked = token_ids - vocab_start
    onehot = (picked[:, None] == jnp.arange(vocab_local, dtype=jnp.int32)[None, :]).astype(
        jnp.bfloat16
    )
    own_rows = lax.psum_scatter(
        jnp.dot(onehot, embed_table, preferred_element_type=jnp.float32),
        ("fsdp", "tp"),
        scatter_dimension=0,
        tiled=True,
    ).astype(jnp.bfloat16)
    embedded = lax.all_gather(own_rows, "tp", axis=0, tiled=True)
    col_width = master_w.shape[1] // count_tp
    whole = lax.all_gather(w_roll, ("fsdp", "tp"), axis=0, tiled=True)
    local_w = lax.dynamic_slice_in_dim(whole, lax.axis_index("tp") * col_width, col_width, 1)
    own_value = jnp.dot(embedded, local_w, preferred_element_type=jnp.float32)
    share = jnp.repeat(residual_mix, HD)[None, :]
    new_value = (share * own_value + (1.0 - share) * first_value.astype(jnp.float32)).astype(
        jnp.bfloat16
    )
    rows = queries.shape[0]
    heads_kv = residual_mix.shape[0]
    group = HEADS // KV
    context = cache_keys.shape[1]
    scale = 1.0 / math.sqrt(HD)
    query_b = queries.reshape(rows, heads_kv, group, HD)
    keys_b = cache_keys.reshape(rows, context, heads_kv, HD)
    vals_b = cache_values.reshape(rows, context, heads_kv, HD)
    newk_b = new_key.reshape(rows, heads_kv, HD)
    newv_b = new_value.reshape(rows, heads_kv, HD)
    scores = (
        jnp.einsum("rkgd,rckd->rkgc", query_b, keys_b, preferred_element_type=jnp.float32) * scale
    )
    fresh = jnp.einsum("rkgd,rkd->rkg", query_b, newk_b, preferred_element_type=jnp.float32) * scale
    valid = jnp.arange(context, dtype=jnp.int32)[None, :] < lengths[:, None]
    scores = jnp.where(valid[:, None, None, :], scores, -1e30)
    peak = jnp.maximum(jnp.max(scores, axis=-1), fresh)
    expo = jnp.exp(scores - peak[..., None])
    expo_new = jnp.exp(fresh - peak)
    total = jnp.sum(expo, axis=-1) + expo_new
    probs = (expo / total[..., None]).astype(jnp.bfloat16)
    probs_new = (expo_new / total).astype(jnp.bfloat16)
    mixed = jnp.einsum("rkgc,rckd->rkgd", probs, vals_b, preferred_element_type=jnp.float32)
    mixed = (
        mixed + probs_new.astype(jnp.float32)[..., None] * newv_b.astype(jnp.float32)[:, :, None, :]
    )
    attended = mixed.reshape(rows, group * heads_kv * HD).astype(jnp.bfloat16)
    return (w_next, new_value, attended)


def solution(mesh):
    return jax.shard_map(
        per_device,
        mesh=mesh,
        in_specs=(
            P(("fsdp", "tp"), None),
            P(("fsdp", "tp"), None),
            P(("fsdp", "tp"), None),
            P(("fsdp", "tp"), None),
            P(),
            P("fsdp", "tp"),
            P("fsdp", None, "tp"),
            P("fsdp", None, "tp"),
            P("fsdp", "tp"),
            P("fsdp", "tp"),
            P("tp"),
            P("fsdp"),
        ),
        out_specs=(P(("fsdp", "tp"), None), P("fsdp", "tp"), P("fsdp", "tp")),
        check_vma=False,
    )
```

profile of v0, /device:TPU:0, one launch (start us, length us, event | category | flops | bytes accessed | tf_op | source)
XLA Modules:
  0.0 832.3 jit_solution(5048618985555372474)
XLA Ops:
  7.2 0.0 copy-start
  7.2 0.0 reduce-scatter.2.cloned.1.call-start
  7.2 12.1 %fusion.47 = f32[5120,1024]{1,0:T(8,128)} fusion(bf16[512,5120]{1,0:T(8,128)(2,1)} %param.12, bf16[512,1024]{1,0:T(8,128)(2,1)} %param.13), kind=kOutput, calls=%fused_computation.45 | convolution fusion | flops 5368709120 | bytes 27262976 | tf_op jit(solution)/shard_map/dot_general | solution.py:33
  19.3 0.0 reduce-scatter.2.cloned.1.call-update
  19.3 0.0 all-gather.3.cloned.1.call-start
  19.4 674.5 %reduce-scatter.2.cloned.1.call-done = f32[40,1024]{1,0:T(8,128)} async-done(((f32[5120,1024]{1,0:T(8,128)}), f32[40,1024]{1,0:T(8,128)}) %reduce-scatter.2.cloned.1.call-update) | async-done | bytes 163856 | tf_op jit(solution)/shard_map/reduce_scatter | solution.py:32
  693.8 0.0 copy-done.1
  693.8 1.6 fusion.45
  695.4 0.0 all-gather.3.cloned.1.call-update
  695.5 10.4 %fusion.8 = f32[256,5120]{1,0:T(8,128)} fusion(bf16[1187,5120]{1,0:T(8,128)(2,1)} %param.15, s32[256]{0:T(256)S(1)} %broadcast_subtract_fusion), kind=kOutput, calls=%fused_computation.9 | convolution fusion | flops 3111953152 | bytes 17398784 | tf_op jit(solution)/shard_map/dot_general | solution.py:50
  706.0 107.8 %all-reduce.2 = bf16[256,5120]{1,0:T(8,128)(2,1)} all-reduce(f32[256,5120]{1,0:T(8,128)} %fusion.8), channel_id=3, replica_groups=mesh['fsdp'=32,'tp'=4] {'fsdp','tp'}, use_global_device_ids=true, to_apply=%region_1.0.clone | all-reduce | flops 1310720 | bytes 7864320
  813.7 0.9 fusion.40
  814.7 5.3 all-gather
  820.0 0.1 iota_compare_fusion.2
  820.1 0.1 fusion.37
  820.2 0.7 fusion.46
  821.0 0.2 fusion.34
  821.2 0.1 bitcast_subtract_fusion
  821.3 0.1 broadcast_bitcast_fusion
  821.4 0.0 all-gather.3.cloned.1.call-done
  821.4 0.0 copy-start.6
  821.4 2.9 bitcast_convert_fusion
  824.4 0.4 fusion.21
  824.8 0.6 copy.57
  (20 shorter events, 0.1 us)
Async XLA Ops:
  7.2 813.1 %copy-start = (bf16[8,512,256]{2,1,0:T(8,128)(2,1)S(1)}, bf16[8,512,256]{2,1,0:T(8,128)(2,1)}, u32[]{:S(2)}) copy-start(bf16[8,512,256]{2,1,0:T(8,128)(2,1)} %param.18) | copy-start | bytes 6291460
  7.2 686.6 %reduce-scatter.2.cloned.1.call-start = ((), (), s32[]{:S(2)}) async-start(), calls=%async_computation.1 | async-start | bytes 21135360 | tf_op jit(solution)/shard_map/reduce_scatter | solution.py:32
  19.3 674.5 %copy-start.1 = (f32[40,1024]{1,0:T(8,128)S(1)}, f32[40,1024]{1,0:T(8,128)}, u32[]{:S(2)}) copy-start(f32[40,1024]{1,0:T(8,128)} %param.14) | copy-start | bytes 491524
  19.3 676.2 %copy-start.4 = (s32[256]{0:T(256)S(1)}, s32[256]{0:T(256)}, u32[]{:S(2)}) copy-start(s32[256]{0:T(256)} %param.16) | copy-start | bytes 3076
  19.3 802.1 %all-gather.3.cloned.1.call-start = ((), (), s32[]{:S(2)}) async-start(), calls=%async_computation.2 | async-start | bytes 10567680 | tf_op jit(solution)/shard_map/all_gather | solution.py:57
  705.9 114.0 %copy-start.5 = (s32[8]{0:T(128)S(1)}, s32[8]{0:T(128)}, u32[]{:S(2)}) copy-start(s32[8]{0:T(128)} %param.23) | copy-start | bytes 100
  705.9 114.1 %copy-start.2 = (bf16[8,2048]{1,0:T(8,128)(2,1)S(1)}, bf16[8,2048]{1,0:T(8,128)(2,1)}, u32[]{:S(2)}) copy-start(bf16[8,2048]{1,0:T(8,128)(2,1)} %param.17) | copy-start | bytes 98308
  706.0 114.1 %copy-start.7 = (bf16[8,256]{1,0:T(8,128)(2,1)S(1)}, bf16[8,256]{1,0:T(8,128)(2,1)}, u32[]{:S(2)}) copy-start(bf16[8,256]{1,0:T(8,128)(2,1)} %param.20) | copy-start | bytes 12292
  813.7 7.5 copy-start.8
  813.7 7.7 copy-start.3
  821.4 3.0 copy-start.6
Sparse Core Ops, SparseCore 0:
  19.4 674.3 reduce-scatter.1
  696.9 66.0 all-gather.2
where the time goes:
time: 834 us; the launch traced here: 832 us
  waiting for transfers between devices  675 us (81%)
  blocking collectives  113 us (14%)
  matrix products  26.8 us (3%)
  between operations  14.1 us (2%)
    reduce_scatter x1, waiting for transfers between devices, per_device(): lax.psum_scatter(lax.dot_general(activations, grad_out, (((0,), (0,)), ((...  674 us
    unnamed x1, blocking collectives  108 us
  transfers between devices with their start and end apart: 2, of which 1 were waited for; matrix products, arithmetic and copies ran while one was open for 2% of the time, Pallas kernels for 0%

commit v1 on v0

v1 whole, which is shorter than its diff:
```python
import functools
import math

import jax
import jax.numpy as jnp
from jax import lax
from jax.experimental import pallas as pl
from jax.experimental.pallas import tpu as pltpu
from jax.sharding import PartitionSpec as P

HEADS = 64
KV = 8
HD = 128
MESH = pl.DeviceIdType.MESH
F32 = jnp.float32
BF16 = jnp.bfloat16
RING = 4
STEPS = 8
BLOCK = 640
CHIP_ROWS = 80
ROWS = 40


def order_of(rel):
    return lax.rem(11 - 2 * rel + lax.div(rel, 2), 4)


def distance_at(step):
    return lax.rem(6 - step + 3 * lax.div(step, 2) + 2 * lax.div(step, 3), 4)


def tdot(a, b):
    return lax.dot_general(a, b, (((0,), (0,)), ((), ())), preferred_element_type=F32)


def kernel(
    coef,
    act,
    gout,
    master,
    table,
    tokens,
    first,
    mix,
    w_out,
    value_out,
    act_o,
    act_p,
    gout_o,
    gout_p,
    tab,
    onehot,
    m80,
    w80,
    w_in,
    ex,
    er,
    send,
    recv_p,
    recv_m,
    recv_cp,
    recv_cm,
    send4,
    recv4,
    send2,
    recv2,
    send3,
    recv3,
    emb,
    t1,
    rt1,
    t2,
    rt2,
    t3,
    rt3,
    s_load,
    s_tab,
    s_gm,
    ps_act,
    pr_act,
    ps_gm,
    pr_gm,
    ps_e,
    pr_e,
    ps_x,
    pr_x,
    ss_p,
    sr_p,
    ss_m,
    sr_m,
    ss_cp,
    sr_cp,
    ss_cm,
    sr_cm,
    rs_s,
    rs_r,
    ds_s,
    ds_r,
):
    fsdp = lax.axis_index("fsdp")
    tp = lax.axis_index("tp")
    my_y = lax.div(fsdp, 8)
    my_x = lax.rem(lax.div(fsdp, 2), 4)
    my_z = lax.rem(fsdp, 2) * 2 + lax.div(tp, 2)
    core = lax.rem(tp, 2)
    other = 1 - core

    def device(y, x, z, c):
        return ((y * 4 + x) * 2 + lax.div(z, 2), lax.rem(z, 2) * 2 + c)

    def along(axis, hop):
        y = lax.rem(my_y + hop, 4) if axis == "y" else my_y
        x = lax.rem(my_x + hop, 4) if axis == "x" else my_x
        z = lax.rem(my_z + hop, 4) if axis == "z" else my_z
        return device(y, x, z, core)

    partner = device(my_y, my_x, my_z, other)
    nxt = {a: along(a, 1) for a in "yxz"}
    far = {a: along(a, 2) for a in "yxz"}
    prv = {a: along(a, 3) for a in "yxz"}

    def remote(src, dst, s_sem, r_sem, target):
        return pltpu.make_async_remote_copy(
            src_ref=src,
            dst_ref=dst,
            send_sem=s_sem,
            recv_sem=r_sem,
            device_id=target,
            device_id_type=MESH,
        )

    def columns(i):
        y = lax.rem(my_y + distance_at(lax.div(i, 2)), 4)
        return pl.ds(pl.multiple_of((y * 2 + lax.rem(i, 2)) * BLOCK, 128), BLOCK)

    def quarter(q, c):
        return pl.ds(pl.multiple_of((2 * q + c) * 256, 128), 256)

    def load_act(i):
        return pltpu.make_async_copy(act.at[:, columns(i)], act_o.at[i], s_load.at[i])

    def load_tab(i):
        return pltpu.make_async_copy(table.at[:, columns(i)], tab.at[i], s_tab.at[i])

    def load_gout(q):
        return pltpu.make_async_copy(
            gout.at[:, quarter(q, core)], gout_o.at[:, pl.ds(q * 256, 256)], s_gm.at[q]
        )

    def load_master(q):
        return pltpu.make_async_copy(
            master.at[:, quarter(q, core)], m80.at[core, :, pl.ds(q * 256, 256)], s_gm.at[2 + q]
        )

    def pass_act(i):
        return remote(act.at[:, columns(i)], act_p.at[i], ps_act.at[i], pr_act.at[i], partner)

    def pass_gout(q):
        return remote(
            gout.at[:, quarter(q, other)],
            gout_p.at[:, pl.ds(q * 256, 256)],
            ps_gm.at[q],
            pr_gm.at[q],
            partner,
        )

    def pass_master(q, c):
        return remote(
            master.at[:, quarter(q, 1 - c)],
            m80.at[c, :, pl.ds(q * 256, 256)],
            ps_gm.at[2 + q],
            pr_gm.at[2 + q],
            partner,
        )

    def pass_e(i):
        return remote(ex.at[i], er.at[i], ps_e.at[i], pr_e.at[i], partner)

    for q in range(2):
        load_gout(q).start()

    @pl.loop(0, STEPS)
    def _(i):
        load_tab(i).start()
        load_act(i).start()

    for q in range(2):
        load_master(q).start()

    barrier = pltpu.get_barrier_semaphore()
    peers = [partner] + [d[a] for d in (nxt, far, prv) for a in "yxz"]
    for peer in peers:
        pl.semaphore_signal(barrier, inc=1, device_id=peer, device_id_type=MESH)
    pl.semaphore_wait(barrier, len(peers))

    for q in range(2):
        pass_gout(q).start()

    @pl.loop(0, STEPS)
    def _(i):
        pass_act(i).start()

    for q in range(2):
        pass_master(q, core).start()

    vocab = tab.shape[1]
    start = (fsdp * 4 + tp) * vocab
    row = lax.broadcasted_iota(jnp.int32, (vocab, 128), 0) + start
    onehot[:, 0:128] = (row == tokens[pl.ds(core, 1), :]).astype(F32).astype(BF16)
    onehot[:, 128:256] = (row == tokens[pl.ds(other, 1), :]).astype(F32).astype(BF16)

    axis1 = ("x", "x", "z", "z")

    def plus1(k, s):
        return remote(
            send.at[k, lax.div(s, 2), s],
            recv_p.at[k, s],
            ss_p.at[k, s],
            sr_p.at[k, s],
            nxt[axis1[k]],
        )

    def minus1(k, s):
        return remote(
            send.at[k, 2 - 2 * lax.div(s, 2), s],
            recv_m.at[k, s],
            ss_m.at[k, s],
            sr_m.at[k, s],
            prv[axis1[k]],
        )

    def plus1c(k, s):
        return remote(
            send.at[k, 1, s], recv_cp.at[k, s], ss_cp.at[k, s], sr_cp.at[k, s], nxt[axis1[k]]
        )

    def minus1c(k, s):
        return remote(
            send.at[k, 2, 2 + s], recv_cm.at[k, s], ss_cm.at[k, s], sr_cm.at[k, s], prv[axis1[k]]
        )

    low, high = pl.ds(0, 2), pl.ds(2, 2)

    def ring(buf, into, r, axis):
        def copy(j, place, half, target):
            return remote(
                buf.at[place, half], into.at[j], rs_s.at[r, j], rs_r.at[r, j], target[axis]
            )

        return (
            copy(0, 0, low, nxt),
            copy(1, 1, high, nxt),
            copy(2, 1, low, nxt),
            copy(3, 0, high, prv),
            copy(4, 2, low, prv),
            copy(5, 2, high, prv),
        )

    def ring_pass(buf, into, copies):
        copies[0].wait_recv()
        buf[1, 0:2] = (buf[1, 0:2].astype(F32) + into[0].astype(F32)).astype(BF16)
        copies[2].start()
        copies[3].wait_recv()
        buf[2, 2:4] = (buf[2, 2:4].astype(F32) + into[3].astype(F32)).astype(BF16)
        copies[5].start()

    def ring_sum(buf, into, copies):
        for j in (1, 2, 4, 5):
            copies[j].wait_recv()
        return (
            buf[3, 0:2].astype(F32) + into[2].astype(F32) + into[4].astype(F32),
            buf[3, 2:4].astype(F32) + into[1].astype(F32) + into[5].astype(F32),
        )

    ring4 = ring(send4, recv4, 0, "y")

    @pl.loop(0, STEPS)
    def _(i):
        s = lax.div(i, 2)
        p = lax.rem(i, 2)
        load_tab(i).wait()
        found = tdot(tab[i], onehot[...])
        ex[i] = found[:, 128:256].astype(BF16)
        pass_e(i).start()

        @pl.when(i == 0)
        def _():
            for q in range(2):
                load_gout(q).wait()
                pass_gout(q).wait_recv()

        load_act(i).wait()
        pass_act(i).wait_recv()
        total = tdot(act_o[i], gout_o[...]) + tdot(act_p[i], gout_p[...])
        for b in range(2):
            ox = order_of(lax.rem(2 * p + b + 4 - my_x, 4))
            for z in range(4):
                oz = order_of(lax.rem(z + 4 - my_z, 4))
                rows = slice((b * 4 + z) * CHIP_ROWS, (b * 4 + z + 1) * CHIP_ROWS)
                for k in range(4):
                    part = total[rows, k * 128 : (k + 1) * 128].astype(BF16)
                    if k < 2:
                        send[k, ox, s, oz] = part
                    else:
                        send[k, oz, s, ox] = part
        pass_e(i).wait_recv()
        both = (found[:, 0:128] + er[i].astype(F32)).astype(BF16)
        for b in range(2):
            ox = order_of(lax.rem(2 * p + b + 4 - my_x, 4))
            for z in range(4):
                oz = order_of(lax.rem(z + 4 - my_z, 4))
                rows = slice((b * 4 + z) * CHIP_ROWS, (b * 4 + z + 1) * CHIP_ROWS)
                send4[s, ox, oz] = both[rows, :]

        @pl.when(p == 1)
        def _():
            for k in range(4):
                plus1(k, s).start()
                minus1(k, s).start()

        @pl.when(i == 1)
        def _():
            ring4[0].start()
            ring4[3].start()

        @pl.when(i == 3)
        def _():
            ring4[1].start()

        @pl.when(i == 5)
        def _():
            ring4[4].start()

    ring_pass(send4, recv4, ring4)

    @pl.loop(0, 2)
    def _(s):
        for k in range(4):
            plus1(k, s).wait_recv()
            send[k, 1, s] = (send[k, 1, s].astype(F32) + recv_p[k, s].astype(F32)).astype(BF16)
            plus1c(k, s).start()
            minus1(k, 2 + s).wait_recv()
            send[k, 2, 2 + s] = (
                send[k, 2, 2 + s].astype(F32) + recv_m[k, 2 + s].astype(F32)
            ).astype(BF16)
            minus1c(k, s).start()

    ring2 = [ring(send2.at[k], recv2.at[k], 1 + k, "y" if k < 4 else "x") for k in range(5)]

    def begin2(k):
        for j in (0, 3, 1, 4):
            ring2[k][j].start()

    top, bottom = ring_sum(send4, recv4, ring4)
    send2[4, 0:2] = top.astype(BF16)
    send2[4, 2:4] = bottom.astype(BF16)
    begin2(4)
    for k in range(4):
        for s in range(4):
            if s < 2:
                plus1c(k, s).wait_recv()
                minus1(k, s).wait_recv()
                extra = recv_cp[k, s].astype(F32) + recv_m[k, s].astype(F32)
            else:
                plus1(k, s).wait_recv()
                minus1c(k, s - 2).wait_recv()
                extra = recv_p[k, s].astype(F32) + recv_cm[k, s - 2].astype(F32)
            send2[k, s] = (send[k, 3, s].astype(F32) + extra).astype(BF16)
        begin2(k)
    for k in (4, 0, 1, 2, 3):
        ring_pass(send2.at[k], recv2.at[k], ring2[k])

    def direct(buf, into, r, axis):
        return (
            remote(buf.at[0], into.at[0], ds_s.at[r, 0], ds_r.at[r, 0], far[axis]),
            remote(buf.at[1], into.at[1], ds_s.at[r, 1], ds_r.at[r, 1], nxt[axis]),
            remote(buf.at[2], into.at[2], ds_s.at[r, 2], ds_r.at[r, 2], prv[axis]),
        )

    def direct_sum(buf, into, copies):
        for copy in copies:
            copy.wait_recv()
        return (buf[3].astype(F32) + into[1].astype(F32)) + (
            into[2].astype(F32) + into[0].astype(F32)
        )

    ring3 = [
        direct(send3.at[k], recv3.at[k], k, "x" if k in (2, 3) else "z") for k in range(5)
    ]
    for k in (4, 0, 1, 2, 3):
        top, bottom = ring_sum(send2.at[k], recv2.at[k], ring2[k])
        send3[k, 0:2] = top.astype(BF16)
        send3[k, 2:4] = bottom.astype(BF16)
        for copy in ring3[k]:
            copy.start()

    mine = direct_sum(send3.at[4], recv3.at[4], ring3[4]).astype(BF16)
    emb[core] = mine
    pass_emb = remote(emb.at[core], emb.at[core], ps_x.at[0], pr_x.at[0], partner)
    pass_emb.start()

    for q in range(2):
        load_master(q).wait()
        pass_master(q, other).wait_recv()
    for k in range(4):
        grad = direct_sum(send3.at[k], recv3.at[k], ring3[k])
        span = slice(k * 128, (k + 1) * 128)
        for c in range(2):
            w80[c, :, span] = m80[c, :, span] - coef * grad[c * ROWS : (c + 1) * ROWS]
    pass_w = remote(w80.at[other], w_in, ps_x.at[1], pr_x.at[1], partner)
    pass_w.start()
    for q in range(2):
        w_out[:, quarter(q, core)] = w80[core, :, q * 256 : (q + 1) * 256]
    w_roll = w80[...].reshape(CHIP_ROWS, 512).astype(BF16)

    remote(emb.at[other], emb.at[other], ps_x.at[0], pr_x.at[0], partner).wait_recv()
    oy = [order_of(lax.rem(y + 4 - my_y, 4)) for y in range(4)]
    ox = [order_of(lax.rem(x + 4 - my_x, 4)) for x in range(4)]
    oz = [order_of(lax.rem(z + 4 - my_z, 4)) for z in range(4)]
    for e in range(2):
        part = tdot(emb[e], w_roll)
        for n in range(16):
            block = e * 16 + n
            y, x, z_hi = block // 8, (block // 2) % 4, block % 2
            for z_lo in range(2):
                z = z_hi * 2 + z_lo
                for h in range(2):
                    lane = (z_lo * 2 + h) * 128
                    piece = part[n * 8 : (n + 1) * 8, lane : lane + 128]
                    if h == 0:
                        t1[h, ox[x], oy[y], oz[z]] = piece
                    else:
                        t1[h, oz[z], oy[y], ox[x]] = piece
    tail = (("x", "y", "z"), ("z", "y", "x"))
    sums = []
    stages = ((t1, rt1), (t2, rt2), (t3, rt3))
    tails = [
        [direct(buf.at[h], into.at[h], 5 + 2 * n + h, tail[h][n]) for h in range(2)]
        for n, (buf, into) in enumerate(stages)
    ]
    for n, (buf, into) in enumerate(stages):
        for h in range(2):
            if n > 0:
                before, came = stages[n - 1]
                buf[h] = direct_sum(before.at[h], came.at[h], tails[n - 1][h])
            for copy in tails[n][h]:
                copy.start()
    for h in range(2):
        own = direct_sum(t3.at[h], rt3.at[h], tails[2][h])
        share = mix[h]
        lane = slice(h * 128, (h + 1) * 128)
        value_out[:, lane] = (
            share * own + (1.0 - share) * first[:, lane].astype(F32)
        ).astype(BF16)

    pass_w.wait_recv()
    for q in range(2):
        w_out[:, quarter(q, other)] = w_in[:, q * 256 : (q + 1) * 256]

    @pl.loop(0, STEPS)
    def _(i):
        pass_act(i).wait_send()
        pass_e(i).wait_send()

    for q in range(2):
        pass_gout(q).wait_send()
        pass_master(q, core).wait_send()
    pass_emb.wait_send()
    pass_w.wait_send()

    @pl.loop(0, 4)
    def _(s):
        for k in range(4):
            plus1(k, s).wait_send()
            minus1(k, s).wait_send()

    @pl.loop(0, 2)
    def _(s):
        for k in range(4):
            plus1c(k, s).wait_send()
            minus1c(k, s).wait_send()

    for copies in [ring4] + ring2 + ring3 + tails[0] + tails[1] + tails[2]:
        for copy in copies:
            copy.wait_send()


def update(activations, grad_out, master_w, embed_table, tokens, first_value, mix, tokens_total):
    width = activations.shape[1]
    vocab = embed_table.shape[0]
    depth = activations.shape[0]
    coef = 1.0 / math.sqrt(tokens_total * width)
    dma = pltpu.SemaphoreType.DMA
    vmem = pltpu.VMEM
    tile = (CHIP_ROWS, 128)
    anywhere = pl.BlockSpec(memory_space=pl.ANY)
    whole = pl.BlockSpec(memory_space=pltpu.VMEM)
    return pl.pallas_call(
        functools.partial(kernel, coef),
        out_shape=(
            jax.ShapeDtypeStruct(master_w.shape, F32),
            jax.ShapeDtypeStruct(first_value.shape, BF16),
        ),
        in_specs=[
            anywhere,
            anywhere,
            anywhere,
            anywhere,
            whole,
            whole,
            pl.BlockSpec(memory_space=pltpu.SMEM),
        ],
        out_specs=(whole, whole),
        scratch_shapes=[
            vmem((STEPS, depth, BLOCK), BF16),
            vmem((STEPS, depth, BLOCK), BF16),
            vmem((depth, 512), BF16),
            vmem((depth, 512), BF16),
            vmem((STEPS, vocab, BLOCK), BF16),
            vmem((vocab, 256), BF16),
            vmem((2, ROWS, 512), F32),
            vmem((2, ROWS, 512), F32),
            vmem((ROWS, 512), F32),
            vmem((STEPS, BLOCK, 128), BF16),
            vmem((STEPS, BLOCK, 128), BF16),
            vmem((4, 4, 4, 4) + tile, BF16),
            vmem((4, 4, 4) + tile, BF16),
            vmem((4, 4, 4) + tile, BF16),
            vmem((4, 2, 4) + tile, BF16),
            vmem((4, 2, 4) + tile, BF16),
            vmem((4, 4, 4) + tile, BF16),
            vmem((6, 2, 4) + tile, BF16),
            vmem((5, 4, 4) + tile, BF16),
            vmem((5, 6, 2) + tile, BF16),
            vmem((5, 4) + tile, BF16),
            vmem((5, 3) + tile, BF16),
            vmem((2,) + tile, BF16),
            vmem((2, 4, 4, 4, 8, 128), F32),
            vmem((2, 3, 4, 4, 8, 128), F32),
            vmem((2, 4, 4, 8, 128), F32),
            vmem((2, 3, 4, 8, 128), F32),
            vmem((2, 4, 8, 128), F32),
            vmem((2, 3, 8, 128), F32),
            dma((STEPS,)),
            dma((STEPS,)),
            dma((4,)),
            dma((STEPS,)),
            dma((STEPS,)),
            dma((4,)),
            dma((4,)),
            dma((STEPS,)),
            dma((STEPS,)),
            dma((2,)),
            dma((2,)),
            dma((4, 4)),
            dma((4, 4)),
            dma((4, 4)),
            dma((4, 4)),
            dma((4, 2)),
            dma((4, 2)),
            dma((4, 2)),
            dma((4, 2)),
            dma((6, 6)),
            dma((6, 6)),
            dma((11, 3)),
            dma((11, 3)),
        ],
        compiler_params=pltpu.CompilerParams(
            collective_id=0, has_side_effects=True, vmem_limit_bytes=60 * 1024 * 1024
        ),
        cost_estimate=pl.CostEstimate(
            flops=2 * depth * width * 1024 + 2 * vocab * width * 256,
            bytes_accessed=2 * width * (depth + vocab),
            transcendentals=0,
        ),
        name="update",
    )(activations, grad_out, master_w, embed_table, tokens, first_value, mix)


def per_device(
    activations,
    grad_out,
    master_w,
    embed_table,
    token_ids,
    queries,
    cache_keys,
    cache_values,
    new_key,
    first_value,
    residual_mix,
    lengths,
):
    devices_all = lax.axis_size("fsdp") * lax.axis_size("tp")
    tokens_total = activations.shape[0] * devices_all
    w_next, new_value = update(
        activations,
        grad_out,
        master_w,
        embed_table,
        token_ids.reshape(2, 128),
        first_value,
        residual_mix,
        tokens_total,
    )
    rows = queries.shape[0]
    heads_kv = residual_mix.shape[0]
    group = HEADS // KV
    context = cache_keys.shape[1]
    scale = 1.0 / math.sqrt(HD)
    query_b = queries.reshape(rows, heads_kv, group, HD)
    keys_b = cache_keys.reshape(rows, context, heads_kv, HD)
    vals_b = cache_values.reshape(rows, context, heads_kv, HD)
    newk_b = new_key.reshape(rows, heads_kv, HD)
    newv_b = new_value.reshape(rows, heads_kv, HD)
    scores = (
        jnp.einsum("rkgd,rckd->rkgc", query_b, keys_b, preferred_element_type=jnp.float32) * scale
    )
    fresh = jnp.einsum("rkgd,rkd->rkg", query_b, newk_b, preferred_element_type=jnp.float32) * scale
    valid = jnp.arange(context, dtype=jnp.int32)[None, :] < lengths[:, None]
    scores = jnp.where(valid[:, None, None, :], scores, -1e30)
    peak = jnp.maximum(jnp.max(scores, axis=-1), fresh)
    expo = jnp.exp(scores - peak[..., None])
    expo_new = jnp.exp(fresh - peak)
    total = jnp.sum(expo, axis=-1) + expo_new
    probs = (expo / total[..., None]).astype(jnp.bfloat16)
    probs_new = (expo_new / total).astype(jnp.bfloat16)
    mixed = jnp.einsum("rkgc,rckd->rkgd", probs, vals_b, preferred_element_type=jnp.float32)
    mixed = (
        mixed + probs_new.astype(jnp.float32)[..., None] * newv_b.astype(jnp.float32)[:, :, None, :]
    )
    attended = mixed.reshape(rows, group * heads_kv * HD).astype(jnp.bfloat16)
    return (w_next, new_value, attended)


def solution(mesh):
    return jax.shard_map(
        per_device,
        mesh=mesh,
        in_specs=(
            P(("fsdp", "tp"), None),
            P(("fsdp", "tp"), None),
            P(("fsdp", "tp"), None),
            P(("fsdp", "tp"), None),
            P(),
            P("fsdp", "tp"),
            P("fsdp", None, "tp"),
            P("fsdp", None, "tp"),
            P("fsdp", "tp"),
            P("fsdp", "tp"),
            P("tp"),
            P("fsdp"),
        ),
        out_specs=(P(("fsdp", "tp"), None), P("fsdp", "tp"), P("fsdp", "tp")),
        check_vma=False,
    )
```

time: 834 us -> 80.4 us (0.10)
  waiting for transfers between devices: 675 us -> 0 us
  blocking collectives: 113 us -> 0 us
  Pallas kernels: 0 us -> 73.5 us
  matrix products: 26.8 us -> 2.08 us
  between operations: 14.1 us -> 0.71 us
    reduce_scatter x1 -> x0, waiting for transfers between devices: 674 us -> none  [per_device(): lax.psum_scatter(lax.dot_general(activations, grad_out, (((0,), (0,)), ((...]
    unnamed x1 -> x0, blocking collectives: 108 us -> none
    pallas_call x0 -> x1, Pallas kernels: none -> 73.5 us  [update(): pl.pallas_call(functools.partial(kernel, coef), out_shape=(jax.ShapeDtype...]
    dot_general x3 -> x0, matrix products: 25.4 us -> none  [the longest x1 12.1 us: per_device(): lax.dot_general(activations, grad_out, (((0,), (0,)), ((), ())), preferre...]
  transfers between devices with their start and end apart: 2 -> 0, of which waited for: 1 -> 0; matrix products, arithmetic and copies ran while one was open for 2% -> 0% of each run, Pallas kernels for 0% -> 0%
where the time goes in v1:
time: 80.4 us; the launch traced here: 80.2 us
  Pallas kernels  73.5 us (91%)
  matrix products  2.08 us (3%)
  local copies, waits for them, and re-layouts  1.93 us (2%)
  other arithmetic  1.93 us (2%)
    pallas_call x1, Pallas kernels, update(): pl.pallas_call(functools.partial(kernel, coef), out_shape=(jax.ShapeDtype...  73.5 us
    unnamed x13, local copies, waits for them, and re-layouts  1.93 us

profile of v1, /device:TPU:0, one launch (start us, length us, event | category | flops | bytes accessed | tf_op | source)
XLA Modules:
  0.0 80.2 jit_solution(661886481375155648)
XLA Ops:
  0.6 0.0 copy-start
  0.6 0.9 %iota_compare_fusion = pred[8,512]{1,0:T(8,128)(4,1)S(1)} fusion(s32[8]{0:T(128)} %param.23), kind=kLoop, calls=%fused_computation.20 | loop fusion | flops 4096 | bytes 4128 | tf_op jit(solution)/shard_map/lt | solution.py:620
  1.5 0.9 %fusion.24 = f32[8,2,1,8]{3,2,1,0:T(1,128)S(1)} fusion(bf16[8,2,8,128]{3,0,2,1:T(8,128)(2,1)} %bitcast.42, bf16[8,2,128,1]{2,0,1,3:T(8,128)(2,1)} %bitcast.47), kind=kOutput, calls=%fused_computation.17 | convolution fusion | flops 32768 | bytes 37376 | tf_op jit(solution)/shard_map/rkgd,rkd->rkg/dot_general | solution.py:619
  2.4 0.0 copy-start.2
  2.4 73.5 %update.1 = (f32[40,1024]{1,0:T(8,128)}, bf16[8,256]{1,0:T(8,128)(2,1)}) custom-call(bf16[512,5120]{1,0:T(8,128)(2,1)} %act.1, bf16[512,1024]{1,0:T(8,128)(2,1)} %gout.1, f32[40,1024]{1,0:T(8,128)} %master.1, bf16[1187,5120]{1,0:T(8,128)(2,1)} %table.1, s32[2,128]{1,0:T(2,128)} %bitcast.48, bf16[8,256]{1,0:T(8,128)(2,1)} %first.1, f32[2]{0:T(128)} %mix.1), custom_call_target="tpu_custom_call" | custom-call | flops 8480358400 | bytes 17397760 | tf_op jit(solution)/shard_map/update/pallas_call | solution.py:498
  76.0 0.0 copy-start.4
  76.0 0.8 %bitcast_convert_fusion = f32[8,2,128]{2,0,1:T(8,128)S(1)} fusion(bf16[8,256]{1,0:T(8,128)(2,1)} %get-tuple-element.15), kind=kLoop, calls=%fused_computation.25 | loop fusion | flops 2048 | bytes 12288 | tf_op jit(solution)/shard_map/convert_element_type | solution.py:630
  76.8 0.0 copy-done
  76.8 0.0 copy-done.2
  76.8 0.7 fusion.30
  77.6 0.0 copy-start.1
  77.6 0.0 copy-start.3
  77.6 0.2 fusion.21
  77.8 0.0 copy-done.4
  77.8 0.4 fusion.18
  78.3 0.6 copy.53
  78.9 0.0 copy-done.1
  78.9 0.7 copy.56
  79.6 0.0 copy-done.3
  79.6 0.6 copy.57
  (3 shorter events, 0.0 us)
Async XLA Ops:
  0.6 76.2 %copy-start = (bf16[8,512,256]{2,1,0:T(8,128)(2,1)S(1)}, bf16[8,512,256]{2,1,0:T(8,128)(2,1)}, u32[]{:S(2)}) copy-start(bf16[8,512,256]{2,1,0:T(8,128)(2,1)} %param.18) | copy-start | bytes 6291460
  2.4 74.4 %copy-start.2 = (bf16[8,2048]{1,0:T(8,128)(2,1)S(1)}, bf16[8,2048]{1,0:T(8,128)(2,1)}, u32[]{:S(2)}) copy-start(bf16[8,2048]{1,0:T(8,128)(2,1)} %param.17) | copy-start | bytes 98308
  76.0 1.9 %copy-start.4 = (bf16[8,512,256]{2,1,0:T(8,128)(2,1)S(1)}, bf16[8,512,256]{2,1,0:T(8,128)(2,1)}, u32[]{:S(2)}) copy-start(bf16[8,512,256]{2,1,0:T(8,128)(2,1)} %param.19) | copy-start | bytes 6291460
  77.6 1.4 %copy-start.1 = (f32[40,1024]{1,0:T(8,128)S(1)}, f32[40,1024]{1,0:T(8,128)}, u32[]{:S(2)}) copy-start(f32[40,1024]{1,0:T(8,128)} %get-tuple-element.14) | copy-start | bytes 491524
  77.6 2.0 %copy-start.3 = (bf16[8,256]{1,0:T(8,128)(2,1)S(1)}, bf16[8,256]{1,0:T(8,128)(2,1)}, u32[]{:S(2)}) copy-start(bf16[8,256]{1,0:T(8,128)(2,1)} %get-tuple-element.15) | copy-start | bytes 12292

commit v2 on v1

v2 whole, which is shorter than its diff:
```python
import functools
import math

import jax
import jax.numpy as jnp
from jax import lax
from jax.experimental import pallas as pl
from jax.experimental.pallas import tpu as pltpu
from jax.sharding import PartitionSpec as P

HD = 128
MESH = pl.DeviceIdType.MESH
F32 = jnp.float32
BF16 = jnp.bfloat16
STEPS = 8
BLOCK = 640
AHEAD = 2
CHIP_ROWS = 80
ROWS = 40
CUT2 = 48
CUT3 = 64
STACK_A = CHIP_ROWS + CUT3
STACK = CHIP_ROWS + CUT2
EDGE = 2 * CHIP_ROWS - CUT2


def order_of(rel):
    return lax.rem(11 - 2 * rel + lax.div(rel, 2), 4)


def distance_at(step):
    return lax.rem(6 - step + 3 * lax.div(step, 2) + 2 * lax.div(step, 3), 4)


def tdot(a, b):
    return lax.dot_general(a, b, (((0,), (0,)), ((), ())), preferred_element_type=F32)


def kernel(
    coef,
    act,
    gout,
    master,
    table,
    keys,
    vals,
    tokens,
    first,
    query,
    new_key,
    mix,
    lengths,
    w_out,
    value_out,
    att_out,
    act_o,
    act_p,
    gout_o,
    gout_p,
    tab,
    onehot,
    keys_v,
    vals_v,
    qs,
    nk,
    mixed,
    fresh_prob,
    m80,
    w80,
    w_in,
    ex,
    er,
    send_a,
    recv_a,
    send_c,
    recv_c,
    send_b,
    recv_b,
    send2_a,
    send2_c,
    recv2_a,
    recv2_c,
    send2_b,
    recv2_b,
    send3_a,
    send3_c,
    recv3_a,
    recv3_c,
    send3_b,
    recv3_b,
    emb,
    t1,
    t1b,
    rt1,
    t2,
    rt2,
    t3,
    rt3,
    s_load,
    s_tab,
    s_gm,
    s_kv,
    ps_act,
    pr_act,
    ps_gm,
    pr_gm,
    ps_e,
    pr_e,
    ps_x,
    pr_x,
    sa_s,
    sa_r,
    sc_s,
    sc_r,
    sb_s,
    sb_r,
    ds_s,
    ds_r,
):
    fsdp = lax.axis_index("fsdp")
    tp = lax.axis_index("tp")
    my_y = lax.div(fsdp, 8)
    my_x = lax.rem(lax.div(fsdp, 2), 4)
    my_z = lax.rem(fsdp, 2) * 2 + lax.div(tp, 2)
    core = lax.rem(tp, 2)
    other = 1 - core

    def device(y, x, z, c):
        return ((y * 4 + x) * 2 + lax.div(z, 2), lax.rem(z, 2) * 2 + c)

    def along(axis, hop):
        y = lax.rem(my_y + hop, 4) if axis == "y" else my_y
        x = lax.rem(my_x + hop, 4) if axis == "x" else my_x
        z = lax.rem(my_z + hop, 4) if axis == "z" else my_z
        return device(y, x, z, core)

    partner = device(my_y, my_x, my_z, other)
    nxt = {a: along(a, 1) for a in "yxz"}
    far = {a: along(a, 2) for a in "yxz"}
    prv = {a: along(a, 3) for a in "yxz"}
    own_rows = pl.ds(pl.multiple_of(core * ROWS, 8), ROWS)
    other_rows = pl.ds(pl.multiple_of(other * ROWS, 8), ROWS)

    def remote(src, dst, s_sem, r_sem, target):
        return pltpu.make_async_remote_copy(
            src_ref=src,
            dst_ref=dst,
            send_sem=s_sem,
            recv_sem=r_sem,
            device_id=target,
            device_id_type=MESH,
        )

    def pair_at(p):
        return lax.rem(lax.div(my_x, 2) + 1 + p, 2)

    def x_order(w):
        x = 2 * pair_at(w // 2 if isinstance(w, int) else lax.div(w, 2)) + w % 2
        return order_of(lax.rem(x + 4 - my_x, 4))

    def columns(i):
        y = lax.rem(my_y + distance_at(lax.div(i, 2)), 4)
        return pl.ds(pl.multiple_of((y * 2 + pair_at(lax.rem(i, 2))) * BLOCK, 128), BLOCK)

    def quarter(q, c):
        return pl.ds(pl.multiple_of((2 * q + c) * 256, 128), 256)

    def load_act(i):
        return pltpu.make_async_copy(act.at[:, columns(i)], act_o.at[i], s_load.at[i])

    def load_tab(i):
        return pltpu.make_async_copy(table.at[:, columns(i)], tab.at[i], s_tab.at[i])

    def load_gout(q):
        return pltpu.make_async_copy(
            gout.at[:, quarter(q, core)], gout_o.at[:, pl.ds(q * 256, 256)], s_gm.at[q]
        )

    def load_master(q):
        return pltpu.make_async_copy(
            master.at[:, quarter(q, core)],
            m80.at[own_rows, pl.ds(q * 256, 256)],
            s_gm.at[2 + q],
        )

    def pass_act(i):
        return remote(act.at[:, columns(i)], act_p.at[i], ps_act.at[i], pr_act.at[i], partner)

    def pass_gout(q):
        return remote(
            gout.at[:, quarter(q, other)],
            gout_p.at[:, pl.ds(q * 256, 256)],
            ps_gm.at[q],
            pr_gm.at[q],
            partner,
        )

    def pass_master(q, rows):
        return remote(
            master.at[:, quarter(q, other)],
            m80.at[rows, pl.ds(q * 256, 256)],
            ps_gm.at[2 + q],
            pr_gm.at[2 + q],
            partner,
        )

    def pass_e(i):
        return remote(ex.at[i, 1], er.at[i], ps_e.at[i], pr_e.at[i], partner)

    load_tab(0).start()
    for q in range(2):
        load_gout(q).start()

    @pl.loop(0, STEPS - 1)
    def _(i):
        load_act(i).start()
        load_tab(i + 1).start()

    load_act(STEPS - 1).start()

    for q in range(2):
        load_master(q).start()
    load_keys = pltpu.make_async_copy(keys, keys_v, s_kv.at[0])
    load_vals = pltpu.make_async_copy(vals, vals_v, s_kv.at[1])
    load_keys.start()
    load_vals.start()

    barrier = pltpu.get_barrier_semaphore()
    peers = [partner] + [d[a] for d in (nxt, far, prv) for a in "yxz"]
    for peer in peers:
        pl.semaphore_signal(barrier, inc=1, device_id=peer, device_id_type=MESH)
    vocab = tab.shape[1]
    start = (fsdp * 4 + tp) * vocab
    place = (lax.broadcasted_iota(jnp.int32, (128, vocab), 1) + start).astype(F32)
    for e, c in ((0, core), (1, other)):
        named = tokens[:, pl.ds(pl.multiple_of(c * 128, 128), 128)].astype(F32)
        named = jnp.broadcast_to(named, (128, 128)).T[:, 0:1]
        onehot[e * 128 : (e + 1) * 128, :] = (place == named).astype(F32).astype(BF16)
    pl.semaphore_wait(barrier, len(peers))

    for q in range(2):
        pass_gout(q).start()
    for i in range(AHEAD):
        pass_act(i).start()

    places = ((0, 0), (1, 1), (1, 0), (0, 1), (2, 0), (2, 1))

    def copy_a(s, j):
        o, half = places[j]
        return remote(
            send_a.at[o, s, pl.ds(2 * half, 2)],
            recv_a.at[s, j],
            sa_s.at[s, j],
            sa_r.at[s, j],
            nxt["x"] if j < 3 else prv["x"],
        )

    def copy_c(i, j):
        o, half = places[j]
        return remote(
            send_c.at[o, lax.div(i, 2), 2 * lax.rem(i, 2) + half],
            recv_c.at[i, j],
            sc_s.at[i, j],
            sc_r.at[i, j],
            nxt["z"] if j < 3 else prv["z"],
        )

    def copy_b(j):
        o, half = places[j]
        return remote(
            send_b.at[o, pl.ds(2 * half, 2)],
            recv_b.at[j],
            sb_s.at[j],
            sb_r.at[j],
            nxt["y"] if j < 3 else prv["y"],
        )

    def added(x, y):
        return (x.astype(F32) + y.astype(F32)).astype(BF16)

    def forward_a(s):
        copy_a(s, 0).wait_recv()
        send_a[1, s, 0:2] = added(send_a[1, s, 0:2], recv_a[s, 0])
        copy_a(s, 2).start()
        copy_a(s, 3).wait_recv()
        send_a[2, s, 2:4] = added(send_a[2, s, 2:4], recv_a[s, 3])
        copy_a(s, 5).start()

    def forward_c(i):
        st, w = lax.div(i, 2), 2 * lax.rem(i, 2)
        copy_c(i, 0).wait_recv()
        send_c[1, st, w] = added(send_c[1, st, w], recv_c[i, 0])
        copy_c(i, 2).start()
        copy_c(i, 3).wait_recv()
        send_c[2, st, w + 1] = added(send_c[2, st, w + 1], recv_c[i, 3])
        copy_c(i, 5).start()

    def look_up(i):
        load_tab(i).wait()
        found = jnp.dot(onehot[...], tab[i], preferred_element_type=F32)
        ex[i, 0] = found[0:128, :].astype(BF16)
        ex[i, 1] = found[128:256, :].astype(BF16)
        pass_e(i).start()

    look_up(0)
    for q in range(2):
        load_gout(q).wait()
        pass_gout(q).wait_recv()

    @pl.loop(0, STEPS)
    def _(i):
        s = lax.div(i, 2)
        p = lax.rem(i, 2)

        @pl.when(i < STEPS - 1)
        def _():
            look_up(i + 1)

        @pl.when(i + AHEAD < STEPS)
        def _():
            pass_act(i + AHEAD).start()

        load_act(i).wait()
        pass_act(i).wait_recv()
        total = tdot(act_o[i], gout_o[...]) + tdot(act_p[i], gout_p[...])
        for b in range(2):
            w = 2 * p + b
            ox = order_of(lax.rem(2 * pair_at(p) + b + 4 - my_x, 4))
            for z in range(4):
                oz = order_of(lax.rem(z + 4 - my_z, 4))
                part = total[(b * 4 + z) * CHIP_ROWS : (b * 4 + z + 1) * CHIP_ROWS, :].astype(BF16)
                send_a[ox, s, oz, 0:CHIP_ROWS] = part[:, 0:128]
                send_a[ox, s, oz, CHIP_ROWS:STACK_A] = part[0:CUT3, 384:512]
                send_c[oz, s, w, 0:CHIP_ROWS] = part[:, 128:256]
                send_c[oz, s, w, CHIP_ROWS:STACK] = part[0:CUT2, 256:384]
                send_b[s, w, oz, CHIP_ROWS:EDGE] = part[CUT2:, 256:384]
                send_b[s, w, oz, EDGE:STACK] = part[CUT3:, 384:512]
        pass_e(i).wait_recv()
        both = (ex[i, 0].astype(F32) + er[i].astype(F32)).T.astype(BF16)
        for b in range(2):
            w = 2 * p + b
            for z in range(4):
                oz = order_of(lax.rem(z + 4 - my_z, 4))
                send_b[s, w, oz, 0:CHIP_ROWS] = both[
                    (b * 4 + z) * CHIP_ROWS : (b * 4 + z + 1) * CHIP_ROWS, :
                ]

        for j in (0, 3, 1, 4):
            copy_c(i, j).start()

        @pl.when(p == 0)
        def _():
            copy_a(s, 0).start()
            copy_a(s, 3).start()

        @pl.when(p == 1)
        def _():
            copy_a(s, 1).start()
            copy_a(s, 4).start()

        for step, j in ((0, 0), (1, 3), (3, 1), (4, 4)):

            @pl.when(i == step)
            def _(j=j):
                copy_b(j).start()

        @pl.when(i >= 2)
        def _():
            forward_c(i - 2)

        @pl.when((i >= 2) & (p == 0))
        def _():
            forward_a(s - 1)

        @pl.when(i == 5)
        def _():
            copy_b(0).wait_recv()
            send_b[1, 0:2] = added(send_b[1, 0:2], recv_b[0])
            copy_b(2).start()

        @pl.when(i == 7)
        def _():
            copy_b(3).wait_recv()
            send_b[2, 2:4] = added(send_b[2, 2:4], recv_b[3])
            copy_b(5).start()

    forward_c(STEPS - 2)
    forward_a(3)
    forward_c(STEPS - 1)
    for q in range(2):
        pass_master(q, own_rows).start()

    heads = query.shape[1] // HD
    group = heads // 2
    for h in range(heads):
        qs[:, h, :] = query[:, h * HD : (h + 1) * HD].astype(F32)
    for g in range(2):
        nk[:, g, :] = new_key[:, g * HD : (g + 1) * HD].astype(F32)
    load_keys.wait()
    load_vals.wait()
    scale = 1.0 / math.sqrt(HD)
    context = keys.shape[1]
    position = lax.broadcasted_iota(jnp.int32, (group, context), 1)

    def attend(r):
        for g in range(2):
            lanes = slice(g * HD, (g + 1) * HD)
            q = qs[r, g * group : (g + 1) * group, :]
            scores = (
                lax.dot_general(
                    q.astype(BF16),
                    keys_v[r, :, lanes],
                    (((1,), (1,)), ((), ())),
                    preferred_element_type=F32,
                )
                * scale
            )
            fresh = jnp.sum(q * nk[r, g : g + 1, :], axis=1, keepdims=True) * scale
            scores = jnp.where(position < lengths[r], scores, -1e30)
            peak = jnp.maximum(jnp.max(scores, axis=1, keepdims=True), fresh)
            expo = jnp.exp(scores - peak)
            expo_new = jnp.exp(fresh - peak)
            norm = jnp.sum(expo, axis=1, keepdims=True) + expo_new
            probs = (expo / norm).astype(BF16)
            probs_new = (expo_new / norm).astype(BF16).astype(F32)
            mixed[r, g * group : (g + 1) * group, :] = jnp.dot(
                probs, vals_v[r, :, lanes], preferred_element_type=F32
            )
            fresh_prob[r, g * group : (g + 1) * group, :] = jnp.broadcast_to(
                probs_new, (group, HD)
            )

    rows_half = keys.shape[0] // 2
    pl.loop(0, rows_half)(attend)

    def direct(buf, into, r, axis):
        return (
            remote(buf.at[0], into.at[0], ds_s.at[r, 0], ds_r.at[r, 0], far[axis]),
            remote(buf.at[1], into.at[1], ds_s.at[r, 1], ds_r.at[r, 1], nxt[axis]),
            remote(buf.at[2], into.at[2], ds_s.at[r, 2], ds_r.at[r, 2], prv[axis]),
        )

    def direct_sum(buf, into, copies):
        for copy in copies:
            copy.wait_recv()
        return (buf[3].astype(F32) + into[1].astype(F32)) + (
            into[2].astype(F32) + into[0].astype(F32)
        )

    stacks2 = (
        (send2_a, recv2_a, direct(send2_a, recv2_a, 0, "y")),
        (send2_c, recv2_c, direct(send2_c, recv2_c, 1, "x")),
        (send2_b, recv2_b, direct(send2_b, recv2_b, 2, "z")),
    )
    stacks3 = (
        (send3_a, recv3_a, direct(send3_a, recv3_a, 3, "z")),
        (send3_c, recv3_c, direct(send3_c, recv3_c, 4, "y")),
        (send3_b, recv3_b, direct(send3_b, recv3_b, 5, "x")),
    )

    def three(x, y, z):
        return (x.astype(F32) + y.astype(F32) + z.astype(F32)).astype(BF16)

    for j in (1, 2, 4, 5):
        copy_b(j).wait_recv()
    for w in range(4):
        v = w % 2
        came = (recv_b[2, v], recv_b[4, v]) if w < 2 else (recv_b[1, v], recv_b[5, v])
        send2_b[:, x_order(w)] = three(send_b[3, w], *came)
    for copy in stacks2[2][2]:
        copy.start()
    for n in range(4):
        for j in (1, 2, 4, 5):
            copy_a(n, j).wait_recv()
        send2_a[n, 0:2] = three(send_a[3, n, 0:2], recv_a[n, 2], recv_a[n, 4])
        send2_a[n, 2:4] = three(send_a[3, n, 2:4], recv_a[n, 1], recv_a[n, 5])
    for copy in stacks2[0][2]:
        copy.start()
    for n in range(STEPS):
        for j in (1, 2, 4, 5):
            copy_c(n, j).wait_recv()
        st, w = n // 2, 2 * (n % 2)
        send2_c[x_order(w), st] = three(send_c[3, st, w], recv_c[n, 2], recv_c[n, 4])
        send2_c[x_order(w + 1), st] = three(send_c[3, st, w + 1], recv_c[n, 1], recv_c[n, 5])
    for copy in stacks2[1][2]:
        copy.start()
    pl.loop(rows_half, keys.shape[0])(attend)

    for k in (2, 0, 1):
        stacks3[k][0][...] = direct_sum(*stacks2[k]).astype(BF16)
        for copy in stacks3[k][2]:
            copy.start()

    sum_b = direct_sum(*stacks3[2])
    emb[core] = sum_b[0:CHIP_ROWS].astype(BF16)
    pass_emb = remote(emb.at[core], emb.at[core], ps_x.at[0], pr_x.at[0], partner)
    pass_emb.start()

    for q in range(2):
        load_master(q).wait()
        pass_master(q, other_rows).wait_recv()
    sum_a = direct_sum(*stacks3[0])
    w80[:, 0:128] = m80[:, 0:128] - coef * sum_a[0:CHIP_ROWS]
    w80[0:CUT3, 384:512] = m80[0:CUT3, 384:512] - coef * sum_a[CHIP_ROWS:STACK_A]
    w80[CUT3:, 384:512] = m80[CUT3:, 384:512] - coef * sum_b[EDGE:STACK]
    sum_c = direct_sum(*stacks3[1])
    w80[:, 128:256] = m80[:, 128:256] - coef * sum_c[0:CHIP_ROWS]
    w80[0:CUT2, 256:384] = m80[0:CUT2, 256:384] - coef * sum_c[CHIP_ROWS:STACK]
    w80[CUT2:, 256:384] = m80[CUT2:, 256:384] - coef * sum_b[CHIP_ROWS:EDGE]
    pass_w = remote(w80.at[other_rows], w_in, ps_x.at[1], pr_x.at[1], partner)
    pass_w.start()
    w_roll = w80[...].astype(BF16)

    remote(emb.at[other], emb.at[other], ps_x.at[0], pr_x.at[0], partner).wait_recv()
    oy = [order_of(lax.rem(y + 4 - my_y, 4)) for y in range(4)]
    ox = [order_of(lax.rem(x + 4 - my_x, 4)) for x in range(4)]
    oz = [order_of(lax.rem(z + 4 - my_z, 4)) for z in range(4)]
    for e in range(2):
        part = tdot(emb[e], w_roll)
        for n in range(16):
            block = e * 16 + n
            y, x, z_hi = block // 8, (block // 2) % 4, block % 2
            for z_lo in range(2):
                z = z_hi * 2 + z_lo
                for h in range(2):
                    lane = (z_lo * 2 + h) * 128
                    piece = part[n * 8 : (n + 1) * 8, lane : lane + 128]
                    if h == 0:
                        t1[h, ox[x], oy[y], oz[z]] = piece
                    else:
                        t1[h, oz[z], oy[y], ox[x]] = piece
    for h in range(2):
        t1b[h] = t1[h].reshape(4, 4, 2, 16, 128).astype(BF16)
    tail = (("x", "y", "z"), ("z", "y", "x"))
    stages = ((t1b, rt1), (t2, rt2), (t3, rt3))
    tails = [
        [direct(buf.at[h], into.at[h], 6 + 2 * n + h, tail[h][n]) for h in range(2)]
        for n, (buf, into) in enumerate(stages)
    ]
    for n, (buf, into) in enumerate(stages):
        for h in range(2):
            if n > 0:
                before, came = stages[n - 1]
                done = direct_sum(before.at[h], came.at[h], tails[n - 1][h])
                buf[h] = done.reshape(buf.shape[1:])
            for copy in tails[n][h]:
                copy.start()
    for q in range(2):
        w_out[:, quarter(q, core)] = w80[own_rows, q * 256 : (q + 1) * 256]
    pass_w.wait_recv()
    for q in range(2):
        w_out[:, quarter(q, other)] = w_in[:, q * 256 : (q + 1) * 256]
    for h in range(2):
        own = direct_sum(t3.at[h], rt3.at[h], tails[2][h])
        share = mix[h]
        lanes = slice(h * HD, (h + 1) * HD)
        value = (share * own + (1.0 - share) * first[:, lanes].astype(F32)).astype(BF16)
        value_out[:, lanes] = value
        fresh_value = value.astype(F32)
        for n in range(h * group, (h + 1) * group):
            att_out[:, n * HD : (n + 1) * HD] = (
                mixed[:, n, :] + fresh_prob[:, n, :] * fresh_value
            ).astype(BF16)

    @pl.loop(0, STEPS)
    def _(i):
        pass_act(i).wait_send()
        pass_e(i).wait_send()

    for q in range(2):
        pass_gout(q).wait_send()
        pass_master(q, own_rows).wait_send()
    pass_emb.wait_send()
    pass_w.wait_send()

    @pl.loop(0, 4)
    def _(s):
        for j in range(6):
            copy_a(s, j).wait_send()

    @pl.loop(0, STEPS)
    def _(i):
        for j in range(6):
            copy_c(i, j).wait_send()

    for j in range(6):
        copy_b(j).wait_send()
    for _, _, copies in stacks2 + stacks3:
        for copy in copies:
            copy.wait_send()
    for stage in tails:
        for copies in stage:
            for copy in copies:
                copy.wait_send()


def update(
    activations,
    grad_out,
    master_w,
    embed_table,
    cache_keys,
    cache_values,
    tokens,
    first_value,
    queries,
    new_key,
    mix,
    lengths,
    tokens_total,
):
    width = activations.shape[1]
    vocab = embed_table.shape[0]
    depth = activations.shape[0]
    rows = queries.shape[0]
    heads = queries.shape[1] // HD
    coef = 1.0 / math.sqrt(tokens_total * width)
    dma = pltpu.SemaphoreType.DMA
    vmem = pltpu.VMEM
    tile = (STACK, 128)
    tile_a = (STACK_A, 128)
    anywhere = pl.BlockSpec(memory_space=pl.ANY)
    whole = pl.BlockSpec(memory_space=pltpu.VMEM)
    scalars = pl.BlockSpec(memory_space=pltpu.SMEM)
    return pl.pallas_call(
        functools.partial(kernel, coef),
        out_shape=(
            jax.ShapeDtypeStruct(master_w.shape, F32),
            jax.ShapeDtypeStruct(first_value.shape, BF16),
            jax.ShapeDtypeStruct(queries.shape, BF16),
        ),
        in_specs=[anywhere] * 6 + [whole] * 4 + [scalars] * 2,
        out_specs=(whole, whole, whole),
        scratch_shapes=[
            vmem((STEPS, depth, BLOCK), BF16),
            vmem((STEPS, depth, BLOCK), BF16),
            vmem((depth, 512), BF16),
            vmem((depth, 512), BF16),
            vmem((STEPS, vocab, BLOCK), BF16),
            vmem((256, vocab), BF16),
            vmem(cache_keys.shape, BF16),
            vmem(cache_values.shape, BF16),
            vmem((rows, heads, HD), F32),
            vmem((rows, 2, HD), F32),
            vmem((rows, heads, HD), F32),
            vmem((rows, heads, HD), F32),
            vmem((CHIP_ROWS, 512), F32),
            vmem((CHIP_ROWS, 512), F32),
            vmem((ROWS, 512), F32),
            vmem((STEPS, 2, 128, BLOCK), BF16),
            vmem((STEPS, 128, BLOCK), BF16),
            vmem((4, 4, 4) + tile_a, BF16),
            vmem((4, 6, 2) + tile_a, BF16),
            vmem((4, 4, 4) + tile, BF16),
            vmem((STEPS, 6) + tile, BF16),
            vmem((4, 4, 4) + tile, BF16),
            vmem((6, 2, 4) + tile, BF16),
            vmem((4, 4) + tile_a, BF16),
            vmem((4, 4) + tile, BF16),
            vmem((3, 4) + tile_a, BF16),
            vmem((3, 4) + tile, BF16),
            vmem((4, 4) + tile, BF16),
            vmem((3, 4) + tile, BF16),
            vmem((4,) + tile_a, BF16),
            vmem((4,) + tile, BF16),
            vmem((3,) + tile_a, BF16),
            vmem((3,) + tile, BF16),
            vmem((4,) + tile, BF16),
            vmem((3,) + tile, BF16),
            vmem((2, CHIP_ROWS, 128), BF16),
            vmem((2, 4, 4, 4, 8, 128), F32),
            vmem((2, 4, 4, 2, 16, 128), BF16),
            vmem((2, 3, 4, 2, 16, 128), BF16),
            vmem((2, 4, 4, 8, 128), F32),
            vmem((2, 3, 4, 8, 128), F32),
            vmem((2, 4, 8, 128), F32),
            vmem((2, 3, 8, 128), F32),
            dma((STEPS,)),
            dma((STEPS,)),
            dma((4,)),
            dma((2,)),
            dma((STEPS,)),
            dma((STEPS,)),
            dma((4,)),
            dma((4,)),
            dma((STEPS,)),
            dma((STEPS,)),
            dma((2,)),
            dma((2,)),
            dma((4, 6)),
            dma((4, 6)),
            dma((STEPS, 6)),
            dma((STEPS, 6)),
            dma((6,)),
            dma((6,)),
            dma((12, 3)),
            dma((12, 3)),
        ],
        compiler_params=pltpu.CompilerParams(
            collective_id=0, has_side_effects=True, vmem_limit_bytes=60 * 1024 * 1024
        ),
        cost_estimate=pl.CostEstimate(
            flops=2 * depth * width * 1024 + 2 * vocab * width * 256,
            bytes_accessed=2 * width * (depth + vocab),
            transcendentals=0,
        ),
        name="update",
    )(
        activations,
        grad_out,
        master_w,
        embed_table,
        cache_keys,
        cache_values,
        tokens,
        first_value,
        queries,
        new_key,
        mix,
        lengths,
    )


def per_device(
    activations,
    grad_out,
    master_w,
    embed_table,
    token_ids,
    queries,
    cache_keys,
    cache_values,
    new_key,
    first_value,
    residual_mix,
    lengths,
):
    devices_all = lax.axis_size("fsdp") * lax.axis_size("tp")
    return update(
        activations,
        grad_out,
        master_w,
        embed_table,
        cache_keys,
        cache_values,
        token_ids.reshape(1, -1),
        first_value,
        queries,
        new_key,
        residual_mix,
        lengths,
        activations.shape[0] * devices_all,
    )


def solution(mesh):
    return jax.shard_map(
        per_device,
        mesh=mesh,
        in_specs=(
            P(("fsdp", "tp"), None),
            P(("fsdp", "tp"), None),
            P(("fsdp", "tp"), None),
            P(("fsdp", "tp"), None),
            P(),
            P("fsdp", "tp"),
            P("fsdp", None, "tp"),
            P("fsdp", None, "tp"),
            P("fsdp", "tp"),
            P("fsdp", "tp"),
            P("tp"),
            P("fsdp"),
        ),
        out_specs=(P(("fsdp", "tp"), None), P("fsdp", "tp"), P("fsdp", "tp")),
        check_vma=False,
    )
```

time: 80.4 us -> 67 us (0.83)
  Pallas kernels: 73.5 us -> 61.9 us
  local copies, waits for them, and re-layouts: 1.93 us -> 4.23 us
  matrix products: 2.08 us -> 0 us
  other arithmetic: 1.93 us -> 0 us
    pallas_call x1, Pallas kernels: 73.5 us -> 61.9 us  [update(): pl.pallas_call(functools.partial(kernel, coef), out_shape=(jax.ShapeDtype...]
    unnamed x13 -> x3, local copies, waits for them, and re-layouts: 1.93 us -> 4.23 us
    dot_general x3 -> x0, matrix products: 2.08 us -> none  [the longest x1 0.9 us: per_device(): jnp.einsum('rkgd,rkd->rkg', query_b, newk_b, preferred_element_type=jnp.f...]
    lt x1 -> x0, other arithmetic: 0.88 us -> none  [per_device(): valid = jnp.arange(context, dtype=jnp.int32)[None, :] < lengths[:, None]]
    convert_element_type x2 -> x0, other arithmetic: 0.85 us -> none  [the longest x1 0.82 us: per_device(): newv_b.astype(jnp.float32)[:, :, None, :]]
where the time goes in v2:
time: 67 us; the launch traced here: 66.7 us
  Pallas kernels  61.9 us (92%)
  local copies, waits for them, and re-layouts  4.23 us (6%)
    pallas_call x1, Pallas kernels, update(): pl.pallas_call(functools.partial(kernel, coef), out_shape=(jax.ShapeDtype...  61.9 us
    unnamed x3, local copies, waits for them, and re-layouts  4.23 us

profile of v2, /device:TPU:0, one launch (start us, length us, event | category | flops | bytes accessed | tf_op | source)
XLA Modules:
  0.0 66.7 jit_solution(1197959306917969645)
XLA Ops:
  0.6 61.9 %update.1 = (f32[40,1024]{1,0:T(8,128)}, bf16[8,256]{1,0:T(8,128)(2,1)}, bf16[8,2048]{1,0:T(8,128)(2,1)}) custom-call(bf16[512,5120]{1,0:T(8,128)(2,1)} %act.1, bf16[512,1024]{1,0:T(8,128)(2,1)} %gout.1, f32[40,1024]{1,0:T(8,128)} %master.1, bf16[1187,5120]{1,0:T(8,128)(2,1)} %table.1, bf16[8,512,256]{2,1,0:T(8,128)(2,1)} %keys.1, ...), custom_call_target="tpu_custom_call" | custom-call | flops 8480358400 | bytes 17397760 | tf_op jit(solution)/shard_map/update/pallas_call | solution.py:625
  62.5 1.6 %copy.18 = f32[40,1024]{1,0:T(8,128)} copy(f32[40,1024]{1,0:T(8,128)} %get-tuple-element.6) | data formatting | bytes 327680
  64.1 1.3 %copy.19 = bf16[8,256]{1,0:T(8,128)(2,1)} copy(bf16[8,256]{1,0:T(8,128)(2,1)} %get-tuple-element.7) | data formatting | bytes 8192
  65.4 1.4 %copy.20 = bf16[8,2048]{1,0:T(8,128)(2,1)} copy(bf16[8,2048]{1,0:T(8,128)(2,1)} %get-tuple-element.8) | data formatting | bytes 65536

commit v3 on v2

--- a/solution.py
+++ b/solution.py
@@ -17,11 +17,11 @@
 AHEAD = 2
 CHIP_ROWS = 80
 ROWS = 40
-CUT2 = 48
+CUT2 = 64
 CUT3 = 64
 STACK_A = CHIP_ROWS + CUT3
-STACK = CHIP_ROWS + CUT2
 EDGE = 2 * CHIP_ROWS - CUT2
+STACK = EDGE + CHIP_ROWS - CUT3
 
 
 def order_of(rel):
@@ -114,6 +114,8 @@
     sc_r,
     sb_s,
     sb_r,
+    sd_s,
+    sd_r,
     ds_s,
     ds_r,
 ):
@@ -207,6 +209,11 @@
     def pass_e(i):
         return remote(ex.at[i, 1], er.at[i], ps_e.at[i], pr_e.at[i], partner)
 
+    barrier = pltpu.get_barrier_semaphore()
+    peers = [partner] + [d[a] for d in (nxt, far, prv) for a in "yxz"]
+    for peer in peers:
+        pl.semaphore_signal(barrier, inc=1, device_id=peer, device_id_type=MESH)
+
     load_tab(0).start()
     for q in range(2):
         load_gout(q).start()
@@ -225,10 +232,6 @@
     load_keys.start()
     load_vals.start()
 
-    barrier = pltpu.get_barrier_semaphore()
-    peers = [partner] + [d[a] for d in (nxt, far, prv) for a in "yxz"]
-    for peer in peers:
-        pl.semaphore_signal(barrier, inc=1, device_id=peer, device_id_type=MESH)
     vocab = tab.shape[1]
     start = (fsdp * 4 + tp) * vocab
     place = (lax.broadcasted_iota(jnp.int32, (128, vocab), 1) + start).astype(F32)
@@ -295,6 +298,65 @@
         send_c[2, st, w + 1] = added(send_c[2, st, w + 1], recv_c[i, 3])
         copy_c(i, 5).start()
 
+    def direct(buf, into, r, axis):
+        return (
+            remote(buf.at[0], into.at[0], ds_s.at[r, 0], ds_r.at[r, 0], far[axis]),
+            remote(buf.at[1], into.at[1], ds_s.at[r, 1], ds_r.at[r, 1], nxt[axis]),
+            remote(buf.at[2], into.at[2], ds_s.at[r, 2], ds_r.at[r, 2], prv[axis]),
+        )
+
+    def direct_sum(buf, into, copies):
+        for copy in copies:
+            copy.wait_recv()
+        return (buf[3].astype(F32) + into[1].astype(F32)) + (
+            into[2].astype(F32) + into[0].astype(F32)
+        )
+
+    stacks2 = (
+        (send2_a, recv2_a, direct(send2_a, recv2_a, 0, "y")),
+        (send2_b, recv2_b, direct(send2_b, recv2_b, 2, "z")),
+    )
+    stacks3 = (
+        (send3_a, recv3_a, direct(send3_a, recv3_a, 3, "z")),
+        (send3_c, recv3_c, direct(send3_c, recv3_c, 4, "y")),
+        (send3_b, recv3_b, direct(send3_b, recv3_b, 5, "x")),
+    )
+
+    pieces = [
+        [
+            remote(
+                send2_c.at[o, n],
+                recv2_c.at[o, n],
+                sd_s.at[n, o],
+                sd_r.at[n, o],
+                (far, nxt, prv)[o]["x"],
+            )
+            for o in range(3)
+        ]
+        for n in range(4)
+    ]
+
+    def three(x, y, z):
+        return (x.astype(F32) + y.astype(F32) + z.astype(F32)).astype(BF16)
+
+    def finish_a(n):
+        for j in (1, 2, 4, 5):
+            copy_a(n, j).wait_recv()
+        send2_a[n, 0:2] = three(send_a[3, n, 0:2], recv_a[n, 2], recv_a[n, 4])
+        send2_a[n, 2:4] = three(send_a[3, n, 2:4], recv_a[n, 1], recv_a[n, 5])
+        if n < 3:
+            stacks2[0][2][n].start()
+
+    def finish_c(st):
+        for n in (2 * st, 2 * st + 1):
+            for j in (1, 2, 4, 5):
+                copy_c(n, j).wait_recv()
+            w = 2 * (n % 2)
+            send2_c[x_order(w), st] = three(send_c[3, st, w], recv_c[n, 2], recv_c[n, 4])
+            send2_c[x_order(w + 1), st] = three(send_c[3, st, w + 1], recv_c[n, 1], recv_c[n, 5])
+        for copy in pieces[st]:
+            copy.start()
+
     def look_up(i):
         load_tab(i).wait()
         found = jnp.dot(onehot[...], tab[i], preferred_element_type=F32)
@@ -311,10 +373,6 @@
     def _(i):
         s = lax.div(i, 2)
         p = lax.rem(i, 2)
-
-        @pl.when(i < STEPS - 1)
-        def _():
-            look_up(i + 1)
 
         @pl.when(i + AHEAD < STEPS)
         def _():
@@ -332,9 +390,22 @@
                 send_a[ox, s, oz, 0:CHIP_ROWS] = part[:, 0:128]
                 send_a[ox, s, oz, CHIP_ROWS:STACK_A] = part[0:CUT3, 384:512]
                 send_c[oz, s, w, 0:CHIP_ROWS] = part[:, 128:256]
-                send_c[oz, s, w, CHIP_ROWS:STACK] = part[0:CUT2, 256:384]
+                send_c[oz, s, w, CHIP_ROWS:STACK_A] = part[0:CUT2, 256:384]
                 send_b[s, w, oz, CHIP_ROWS:EDGE] = part[CUT2:, 256:384]
                 send_b[s, w, oz, EDGE:STACK] = part[CUT3:, 384:512]
+        for j in (0, 3, 1, 4):
+            copy_c(i, j).start()
+
+        @pl.when(p == 0)
+        def _():
+            copy_a(s, 0).start()
+            copy_a(s, 3).start()
+
+        @pl.when(p == 1)
+        def _():
+            copy_a(s, 1).start()
+            copy_a(s, 4).start()
+
         pass_e(i).wait_recv()
         both = (ex[i, 0].astype(F32) + er[i].astype(F32)).T.astype(BF16)
         for b in range(2):
@@ -345,25 +416,16 @@
                     (b * 4 + z) * CHIP_ROWS : (b * 4 + z + 1) * CHIP_ROWS, :
                 ]
 
-        for j in (0, 3, 1, 4):
-            copy_c(i, j).start()
-
-        @pl.when(p == 0)
-        def _():
-            copy_a(s, 0).start()
-            copy_a(s, 3).start()
-
-        @pl.when(p == 1)
-        def _():
-            copy_a(s, 1).start()
-            copy_a(s, 4).start()
-
         for step, j in ((0, 0), (1, 3), (3, 1), (4, 4)):
 
             @pl.when(i == step)
             def _(j=j):
                 copy_b(j).start()
 
+        @pl.when(i < STEPS - 1)
+        def _():
+            look_up(i + 1)
+
         @pl.when(i >= 2)
         def _():
             forward_c(i - 2)
@@ -372,23 +434,27 @@
         def _():
             forward_a(s - 1)
 
-        @pl.when(i == 5)
+        @pl.when(i == 4)
         def _():
             copy_b(0).wait_recv()
             send_b[1, 0:2] = added(send_b[1, 0:2], recv_b[0])
             copy_b(2).start()
 
-        @pl.when(i == 7)
+        @pl.when(i == 6)
         def _():
             copy_b(3).wait_recv()
             send_b[2, 2:4] = added(send_b[2, 2:4], recv_b[3])
             copy_b(5).start()
+            finish_a(0)
+            finish_c(0)
 
     forward_c(STEPS - 2)
     forward_a(3)
     forward_c(STEPS - 1)
     for q in range(2):
         pass_master(q, own_rows).start()
+    finish_a(1)
+    finish_c(1)
 
     heads = query.shape[1] // HD
     group = heads // 2
@@ -430,66 +496,56 @@
                 probs_new, (group, HD)
             )
 
-    rows_half = keys.shape[0] // 2
-    pl.loop(0, rows_half)(attend)
-
-    def direct(buf, into, r, axis):
-        return (
-            remote(buf.at[0], into.at[0], ds_s.at[r, 0], ds_r.at[r, 0], far[axis]),
-            remote(buf.at[1], into.at[1], ds_s.at[r, 1], ds_r.at[r, 1], nxt[axis]),
-            remote(buf.at[2], into.at[2], ds_s.at[r, 2], ds_r.at[r, 2], prv[axis]),
-        )
-
-    def direct_sum(buf, into, copies):
-        for copy in copies:
-            copy.wait_recv()
-        return (buf[3].astype(F32) + into[1].astype(F32)) + (
-            into[2].astype(F32) + into[0].astype(F32)
-        )
-
-    stacks2 = (
-        (send2_a, recv2_a, direct(send2_a, recv2_a, 0, "y")),
-        (send2_c, recv2_c, direct(send2_c, recv2_c, 1, "x")),
-        (send2_b, recv2_b, direct(send2_b, recv2_b, 2, "z")),
-    )
-    stacks3 = (
-        (send3_a, recv3_a, direct(send3_a, recv3_a, 3, "z")),
-        (send3_c, recv3_c, direct(send3_c, recv3_c, 4, "y")),
-        (send3_b, recv3_b, direct(send3_b, recv3_b, 5, "x")),
-    )
-
-    def three(x, y, z):
-        return (x.astype(F32) + y.astype(F32) + z.astype(F32)).astype(BF16)
-
+    cuts = [keys.shape[0] * n // 8 for n in (0, 2, 4, 6, 8)]
+
+    finish_a(2)
+    finish_c(2)
     for j in (1, 2, 4, 5):
         copy_b(j).wait_recv()
     for w in range(4):
         v = w % 2
         came = (recv_b[2, v], recv_b[4, v]) if w < 2 else (recv_b[1, v], recv_b[5, v])
         send2_b[:, x_order(w)] = three(send_b[3, w], *came)
-    for copy in stacks2[2][2]:
-        copy.start()
-    for n in range(4):
-        for j in (1, 2, 4, 5):
-            copy_a(n, j).wait_recv()
-        send2_a[n, 0:2] = three(send_a[3, n, 0:2], recv_a[n, 2], recv_a[n, 4])
-        send2_a[n, 2:4] = three(send_a[3, n, 2:4], recv_a[n, 1], recv_a[n, 5])
-    for copy in stacks2[0][2]:
-        copy.start()
-    for n in range(STEPS):
-        for j in (1, 2, 4, 5):
-            copy_c(n, j).wait_recv()
-        st, w = n // 2, 2 * (n % 2)
-        send2_c[x_order(w), st] = three(send_c[3, st, w], recv_c[n, 2], recv_c[n, 4])
-        send2_c[x_order(w + 1), st] = three(send_c[3, st, w + 1], recv_c[n, 1], recv_c[n, 5])
     for copy in stacks2[1][2]:
         copy.start()
-    pl.loop(rows_half, keys.shape[0])(attend)
-
-    for k in (2, 0, 1):
-        stacks3[k][0][...] = direct_sum(*stacks2[k]).astype(BF16)
-        for copy in stacks3[k][2]:
-            copy.start()
+    finish_a(3)
+    finish_c(3)
+    pl.loop(cuts[0], cuts[1])(attend)
+
+    @pl.loop(0, STEPS)
+    def _(i):
+        pass_act(i).wait_send()
+        pass_e(i).wait_send()
+        for j in range(6):
+            copy_c(i, j).wait_send()
+
+    @pl.loop(0, 4)
+    def _(s):
+        for j in range(6):
+            copy_a(s, j).wait_send()
+
+    for j in range(6):
+        copy_b(j).wait_send()
+    for q in range(2):
+        pass_gout(q).wait_send()
+        pass_master(q, own_rows).wait_send()
+
+    send3_a[...] = direct_sum(*stacks2[0]).astype(BF16)
+    for copy in stacks3[0][2]:
+        copy.start()
+    send3_b[...] = direct_sum(*stacks2[1]).astype(BF16)
+    for copy in stacks3[2][2]:
+        copy.start()
+    for copies in pieces:
+        for copy in copies:
+            copy.wait_recv()
+    send3_c[...] = (
+        (send2_c[3].astype(F32) + recv2_c[1].astype(F32))
+        + (recv2_c[2].astype(F32) + recv2_c[0].astype(F32))
+    ).astype(BF16)
+    for copy in stacks3[1][2]:
+        copy.start()
+    pl.loop(cuts[1], cuts[2])(attend)
 
     sum_b = direct_sum(*stacks3[2])
     emb[core] = sum_b[0:CHIP_ROWS].astype(BF16)
@@ -505,7 +561,7 @@
     w80[CUT3:, 384:512] = m80[CUT3:, 384:512] - coef * sum_b[EDGE:STACK]
     sum_c = direct_sum(*stacks3[1])
     w80[:, 128:256] = m80[:, 128:256] - coef * sum_c[0:CHIP_ROWS]
-    w80[0:CUT2, 256:384] = m80[0:CUT2, 256:384] - coef * sum_c[CHIP_ROWS:STACK]
+    w80[0:CUT2, 256:384] = m80[0:CUT2, 256:384] - coef * sum_c[CHIP_ROWS:STACK_A]
     w80[CUT2:, 256:384] = m80[CUT2:, 256:384] - coef * sum_b[CHIP_ROWS:EDGE]
     pass_w = remote(w80.at[other_rows], w_in, ps_x.at[1], pr_x.at[1], partner)
     pass_w.start()
@@ -545,6 +601,16 @@
                 buf[h] = done.reshape(buf.shape[1:])
             for copy in tails[n][h]:
                 copy.start()
+        if n < 2:
+            pl.loop(cuts[2 + n], cuts[3 + n])(attend)
+    for _, _, copies in stacks2 + stacks3:
+        for copy in copies:
+            copy.wait_send()
+    for copies in pieces:
+        for copy in copies:
+            copy.wait_send()
+    pass_emb.wait_send()
+    pass_w.wait_send()
     for q in range(2):
         w_out[:, quarter(q, core)] = w80[own_rows, q * 256 : (q + 1) * 256]
     pass_w.wait_recv()
@@ -562,32 +628,6 @@
                 mixed[:, n, :] + fresh_prob[:, n, :] * fresh_value
             ).astype(BF16)
 
-    @pl.loop(0, STEPS)
-    def _(i):
-        pass_act(i).wait_send()
-        pass_e(i).wait_send()
-
-    for q in range(2):
-        pass_gout(q).wait_send()
-        pass_master(q, own_rows).wait_send()
-    pass_emb.wait_send()
-    pass_w.wait_send()
-
-    @pl.loop(0, 4)
-    def _(s):
-        for j in range(6):
-            copy_a(s, j).wait_send()
-
-    @pl.loop(0, STEPS)
-    def _(i):
-        for j in range(6):
-            copy_c(i, j).wait_send()
-
-    for j in range(6):
-        copy_b(j).wait_send()
-    for _, _, copies in stacks2 + stacks3:
-        for copy in copies:
-            copy.wait_send()
     for stage in tails:
         for copies in stage:
             for copy in copies:
@@ -625,9 +665,9 @@
     return pl.pallas_call(
         functools.partial(kernel, coef),
         out_shape=(
-            jax.ShapeDtypeStruct(master_w.shape, F32),
-            jax.ShapeDtypeStruct(first_value.shape, BF16),
-            jax.ShapeDtypeStruct(queries.shape, BF16),
+            vmem(master_w.shape, F32),
+            vmem(first_value.shape, BF16),
+            vmem(queries.shape, BF16),
         ),
         in_specs=[anywhere] * 6 + [whole] * 4 + [scalars] * 2,
         out_specs=(whole, whole, whole),
@@ -651,20 +691,20 @@
             vmem((STEPS, 128, BLOCK), BF16),
             vmem((4, 4, 4) + tile_a, BF16),
             vmem((4, 6, 2) + tile_a, BF16),
-            vmem((4, 4, 4) + tile, BF16),
-            vmem((STEPS, 6) + tile, BF16),
+            vmem((4, 4, 4) + tile_a, BF16),
+            vmem((STEPS, 6) + tile_a, BF16),
             vmem((4, 4, 4) + tile, BF16),
             vmem((6, 2, 4) + tile, BF16),
             vmem((4, 4) + tile_a, BF16),
-            vmem((4, 4) + tile, BF16),
+            vmem((4, 4) + tile_a, BF16),
             vmem((3, 4) + tile_a, BF16),
-            vmem((3, 4) + tile, BF16),
+            vmem((3, 4) + tile_a, BF16),
             vmem((4, 4) + tile, BF16),
             vmem((3, 4) + tile, BF16),
             vmem((4,) + tile_a, BF16),
-            vmem((4,) + tile, BF16),
+            vmem((4,) + tile_a, BF16),
             vmem((3,) + tile_a, BF16),
-            vmem((3,) + tile, BF16),
+            vmem((3,) + tile_a, BF16),
             vmem((4,) + tile, BF16),
             vmem((3,) + tile, BF16),
             vmem((2, CHIP_ROWS, 128), BF16),
@@ -693,6 +733,8 @@
             dma((STEPS, 6)),
             dma((6,)),
             dma((6,)),
+            dma((4, 3)),
+            dma((4, 3)),
             dma((12, 3)),
             dma((12, 3)),
         ],

time: 67 us -> 61.4 us (0.916)
  Pallas kernels: 61.9 us -> 58.7 us
  local copies, waits for them, and re-layouts: 4.23 us -> 1.88 us
    pallas_call x1, Pallas kernels: 61.9 us -> 58.7 us  [update(): pl.pallas_call(functools.partial(kernel, coef), out_shape=(vmem(master_w....]
    unnamed x3, local copies, waits for them, and re-layouts: 4.23 us -> 1.88 us
where the time goes in v3:
time: 61.4 us; the launch traced here: 61.2 us
  Pallas kernels  58.7 us (96%)
  local copies, waits for them, and re-layouts  1.88 us (3%)
  between operations  0.64 us (1%)
    pallas_call x1, Pallas kernels, update(): pl.pallas_call(functools.partial(kernel, coef), out_shape=(vmem(master_w....  58.7 us
    unnamed x3, local copies, waits for them, and re-layouts  1.88 us

profile of v3, /device:TPU:0, one launch (start us, length us, event | category | flops | bytes accessed | tf_op | source)
XLA Modules:
  0.0 61.2 jit_solution(8644438844012886510)
XLA Ops:
  0.6 58.7 %update.1 = (f32[40,1024]{1,0:T(8,128)S(1)}, bf16[8,256]{1,0:T(8,128)(2,1)S(1)}, bf16[8,2048]{1,0:T(8,128)(2,1)S(1)}) custom-call(bf16[512,5120]{1,0:T(8,128)(2,1)} %act.1, bf16[512,1024]{1,0:T(8,128)(2,1)} %gout.1, f32[40,1024]{1,0:T(8,128)} %master.1, bf16[1187,5120]{1,0:T(8,128)(2,1)} %table.1, bf16[8,512,256]{2,1,0:T(8,128)(2,1)} %keys.1, ...), custom_call_target="tpu_custom_call" | custom-call | flops 8480358400 | bytes 17397760 | tf_op jit(solution)/shard_map/update/pallas_call | solution.py:665
  59.3 0.7 %copy.18 = f32[40,1024]{1,0:T(8,128)} copy(f32[40,1024]{1,0:T(8,128)S(1)} %get-tuple-element.3) | data formatting | bytes 327680
  60.0 0.6 copy.19
  60.6 0.6 %copy.20 = bf16[8,2048]{1,0:T(8,128)(2,1)} copy(bf16[8,2048]{1,0:T(8,128)(2,1)S(1)} %get-tuple-element.5) | data formatting | bytes 65536

commit v4 on v3

--- a/solution.py
+++ b/solution.py
@@ -499,7 +499,6 @@
     cuts = [keys.shape[0] * n // 8 for n in (0, 2, 4, 6, 8)]
 
     finish_a(2)
-    finish_c(2)
     for j in (1, 2, 4, 5):
         copy_b(j).wait_recv()
     for w in range(4):
@@ -508,6 +507,7 @@
         send2_b[:, x_order(w)] = three(send_b[3, w], *came)
     for copy in stacks2[1][2]:
         copy.start()
+    finish_c(2)
     finish_a(3)
     finish_c(3)
     pl.loop(cuts[0], cuts[1])(attend)
@@ -530,11 +530,11 @@
         pass_gout(q).wait_send()
         pass_master(q, own_rows).wait_send()
 
+    send3_b[...] = direct_sum(*stacks2[1]).astype(BF16)
+    for copy in stacks3[2][2]:
+        copy.start()
     send3_a[...] = direct_sum(*stacks2[0]).astype(BF16)
     for copy in stacks3[0][2]:
-        copy.start()
-    send3_b[...] = direct_sum(*stacks2[1]).astype(BF16)
-    for copy in stacks3[2][2]:
         copy.start()
     for copies in pieces:
         for copy in copies:
@@ -585,8 +585,6 @@
                         t1[h, ox[x], oy[y], oz[z]] = piece
                     else:
                         t1[h, oz[z], oy[y], ox[x]] = piece
-    for h in range(2):
-        t1b[h] = t1[h].reshape(4, 4, 2, 16, 128).astype(BF16)
     tail = (("x", "y", "z"), ("z", "y", "x"))
     stages = ((t1b, rt1), (t2, rt2), (t3, rt3))
     tails = [
@@ -595,7 +593,9 @@
     ]
     for n, (buf, into) in enumerate(stages):
         for h in range(2):
-            if n > 0:
+            if n == 0:
+                t1b[h] = t1[h].reshape(4, 4, 2, 16, 128).astype(BF16)
+            else:
                 before, came = stages[n - 1]
                 done = direct_sum(before.at[h], came.at[h], tails[n - 1][h])
                 buf[h] = done.reshape(buf.shape[1:])

time: 61.4 us -> 61.1 us (level)
  no operation moved by 1% of the time
where the time goes in v4:
time: 61.1 us; the launch traced here: 61 us
  Pallas kernels  58.4 us (96%)
  local copies, waits for them, and re-layouts  1.88 us (3%)
  between operations  0.64 us (1%)
    pallas_call x1, Pallas kernels, update(): pl.pallas_call(functools.partial(kernel, coef), out_shape=(vmem(master_w....  58.4 us
    unnamed x3, local copies, waits for them, and re-layouts  1.88 us

profile of v4, /device:TPU:0, one launch (start us, length us, event | category | flops | bytes accessed | tf_op | source)
XLA Modules:
  0.0 61.0 jit_solution(13085274784474781155)
XLA Ops:
  0.6 58.4 %update.1 = (f32[40,1024]{1,0:T(8,128)S(1)}, bf16[8,256]{1,0:T(8,128)(2,1)S(1)}, bf16[8,2048]{1,0:T(8,128)(2,1)S(1)}) custom-call(bf16[512,5120]{1,0:T(8,128)(2,1)} %act.1, bf16[512,1024]{1,0:T(8,128)(2,1)} %gout.1, f32[40,1024]{1,0:T(8,128)} %master.1, bf16[1187,5120]{1,0:T(8,128)(2,1)} %table.1, bf16[8,512,256]{2,1,0:T(8,128)(2,1)} %keys.1, ...), custom_call_target="tpu_custom_call" | custom-call | flops 8480358400 | bytes 17397760 | tf_op jit(solution)/shard_map/update/pallas_call | solution.py:665
  59.1 0.7 %copy.18 = f32[40,1024]{1,0:T(8,128)} copy(f32[40,1024]{1,0:T(8,128)S(1)} %get-tuple-element.3) | data formatting | bytes 327680
  59.8 0.6 copy.19
  60.3 0.6 %copy.20 = bf16[8,2048]{1,0:T(8,128)(2,1)} copy(bf16[8,2048]{1,0:T(8,128)(2,1)S(1)} %get-tuple-element.5) | data formatting | bytes 65536
